TPU v7x, 32 devices: a whole 2x2x4 slice. The times are simulated.
32 devices in a mesh: dp: 8 (over z, x), bank: 4 (over y, core).
Axes of the slice: x: 2, y: 2, z: 4, core: 2. Of those that a mesh axis runs over, the one named last changes fastest.
Arguments:
- features: float32 [128, 128], P('dp'), may hold values from -6 to 6
- video_ids: int32 [8, 16], P('dp'), may hold values from 0 to 4, never falling along the last dimension, each value on 1 to 8 neighbouring positions
- bank: float32 [16384, 128], P(('dp', 'bank')), may hold values from -6 to 6
- loss_weight: float32 [128], P('dp'), may hold values from 0.5 to 2
Outputs:
- loss: float32 [128], P('dp')
- feature_grad: float32 [128, 128], P('dp')
Inputs may be any that keep to these rules, and one draw needn't show every extreme that they name: `video_ids`: each row of 16 frames holds 5 videos as runs of equal ids in ascending order, each video 1 to 8 frames and one exactly 8.
All inputs are finite; a program needn't handle non-finite values.
Results may differ from a plain program's by a relative error of at most 0.0003.
Values sent between devices are 32-bit elements; how exact they have to be, the bound alone decides.
A program may use at most 64 MiB of HBM per device.

v0:
```python
import math
import jax
import jax.numpy as jnp
from jax import lax
from jax.sharding import PartitionSpec as P

EPSILON = 1e-06
TAU_BACK = 0.1
HIGHEST = lax.Precision.HIGHEST


def unit_rows(values):
    return values / jnp.sqrt(jnp.sum(values * values, axis=1, keepdims=True) + EPSILON)


def cycle_loss(neighbour, normed, videos):
    frames = videos.shape[0]
    same_video = videos[:, None] == videos[None, :]
    row_index = lax.broadcasted_iota(jnp.int32, (frames, frames), 0)
    col_index = lax.broadcasted_iota(jnp.int32, (frames, frames), 1)
    earlier = same_video & (col_index < row_index)
    position = jnp.sum(jnp.where(earlier, 1.0, 0.0), axis=1).astype(neighbour.dtype)
    products = jnp.dot(neighbour, normed.T, precision=HIGHEST)
    distance = (
        jnp.sum(neighbour * neighbour, axis=1)[:, None]
        - 2.0 * products
        + jnp.sum(normed * normed, axis=1)[None, :]
    )
    back_weight = jnp.where(same_video, jnp.exp(-distance / TAU_BACK), 0.0)
    back_weight = back_weight / jnp.sum(back_weight, axis=1, keepdims=True)
    mean_pos = jnp.dot(back_weight, position, precision=HIGHEST)
    square_pos = jnp.dot(back_weight, position * position, precision=HIGHEST)
    spread = jnp.maximum(square_pos - mean_pos * mean_pos, 1.0)
    return (position - mean_pos) ** 2 / spread + 0.5 * jnp.log(spread)


def reduce_owner(partials):
    whole = lax.psum(partials, "bank")
    return lax.psum_scatter(whole, "dp", scatter_dimension=0, tiled=True)


def shards(features, video_ids, bank, loss_weight):
    per_owner, width = features.shape
    owners = lax.axis_size("dp")
    sharpness = 3.0 * math.sqrt(width)
    lengths = jnp.sqrt(jnp.sum(features * features, axis=1, keepdims=True) + EPSILON)
    normed = features / lengths
    keys = unit_rows(bank)
    gathered = lax.all_gather(normed, "dp", axis=0, tiled=True)
    group = 1
    while owners % (group * 2) == 0 and per_owner * group * 2 <= 512:
        group = group * 2
    step_rows = per_owner * group
    query_blocks = gathered.reshape(-1, step_rows, width)

    def forward_block(query_block):
        exp_scores = jnp.exp(sharpness * jnp.dot(query_block, keys.T, precision=HIGHEST))
        return (jnp.dot(exp_scores, keys, precision=HIGHEST), jnp.sum(exp_scores, axis=1))

    summed, partition = lax.map(forward_block, query_blocks)
    summed, partition = reduce_owner((summed.reshape(-1, width), partition.reshape(-1)))
    neighbour = summed / partition[:, None]
    loss, pullback = jax.vjp(
        lambda soft_rows, unit_part: cycle_loss(soft_rows, unit_part, video_ids[0]),
        neighbour,
        normed,
    )
    grad_soft, grad_local = pullback(loss_weight)
    gathered_grad = lax.all_gather(grad_soft, "dp", axis=0, tiled=True)
    grad_blocks = gathered_grad.reshape(-1, step_rows, width)

    def backward_block(paired):
        query_block, grad_block = paired
        exp_scores = jnp.exp(sharpness * jnp.dot(query_block, keys.T, precision=HIGHEST))
        projected = jnp.dot(grad_block, keys.T, precision=HIGHEST)
        return jnp.dot(exp_scores * projected, keys, precision=HIGHEST)

    moment = lax.map(backward_block, (query_blocks, grad_blocks)).reshape(-1, width)
    moment = reduce_owner((moment,))[0]
    along = jnp.sum(grad_soft * neighbour, axis=1, keepdims=True)
    grad_unit = grad_local + sharpness * (moment / partition[:, None] - along * neighbour)
    feature_grad = (
        grad_unit - normed * jnp.sum(normed * grad_unit, axis=1, keepdims=True)
    ) / lengths
    return (loss, feature_grad)


def solution(mesh):
    return jax.shard_map(
        shards,
        mesh=mesh,
        in_specs=(P("dp", None), P("dp", None), P(("dp", "bank"), None), P("dp")),
        out_specs=(P("dp"), P("dp", None)),
        check_vma=False,
    )
```

profile of v0, /device:TPU:0, one launch (start us, length us, event | category | flops | bytes accessed | tf_op | source)
XLA Modules:
  0.0 221.4 jit_solution(16359548754769475887)
XLA Ops:
  7.2 0.0 reduce-scatter.3.cloned.1.call-start
  7.2 0.8 multiply_reduce_fusion.6
  8.1 1.1 multiply_reduce_fusion
  9.2 0.2 multiply_reduce_fusion.4
  9.4 32.3 %all_gather.6 = f32[128,128]{1,0:T(8,128)S(1)} all-gather(f32[16,128]{1,0:T(8,128)S(1)} %get-tuple-element.42), channel_id=1, replica_groups=mesh['dp'=8,'bank'=4] {'dp'}, dimensions={0}, use_global_device_ids=true | all-gather | bytes 73728 | tf_op jit(solution)/shard_map/all_gather | solution.py:49
  41.7 0.6 fusion.28
  42.3 1.1 fusion.25
  43.4 0.0 reduce-scatter.3.cloned.1.call-update
  43.4 0.0 reduce-scatter.5.cloned.1.call-start
  43.5 0.6 copy-done.4
  44.1 0.6 dynamic-slice.2
  45.3 21.3 %all-reduce = f32[128]{0:T(128)S(1)} all-reduce(f32[128]{0:T(128)S(1)} %get-tuple-element.45), channel_id=3, replica_groups=mesh['dp'=8,'bank'=4] {'dp'}, use_global_device_ids=true, to_apply=%region_7.8.clone | all-reduce | flops 128 | bytes 1024
  66.7 0.1 dynamic-slice.3
  66.7 39.0 %reduce-scatter.3.cloned.1.call-done = f32[16,128]{1,0:T(8,128)} async-done(((f32[128,128]{1,0:T(8,128)}), f32[16,128]{1,0:T(8,128)}) %reduce-scatter.3.cloned.1.call-update) | async-done | bytes 8208 | tf_op jit(solution)/shard_map/reduce_scatter | solution.py:39
  105.7 6.0 %all-reduce.1 = (f32[16,128]{1,0:T(8,128)S(1)}, f32[16]{0:T(128)S(1)}) all-reduce(f32[16,128]{1,0:T(8,128)} %reduce-scatter.3.cloned.1.call-done, f32[16]{0:T(128)S(1)} %dynamic-slice.3), channel_id=1, replica_groups=mesh['dp'=8,'bank'=4] {'bank'}, use_global_device_ids=true, to_apply=%region_3.0 | all-reduce | flops 2064 | bytes 16512 | tf_op jit(solution)/shard_map/psum | solution.py:38
  111.7 0.2 multiply_reduce_fusion.5
  111.9 0.7 copy-done.2
  112.6 0.2 fusion.12
  112.8 0.2 convolution_bitcast_fusion.1
  113.0 0.5 copy-done.3
  113.5 0.7 add_add_fusion
  114.2 0.1 multiply_reduce_fusion.3
  114.3 0.2 multiply_reduce_fusion.8
  114.5 0.3 multiply_reduce_fusion.2
  114.8 30.5 %all_gather.7 = f32[128,128]{1,0:T(8,128)S(1)} all-gather(f32[16,128]{1,0:T(8,128)S(1)} %get-tuple-element.49), channel_id=1, replica_groups=mesh['dp'=8,'bank'=4] {'dp'}, dimensions={0}, use_global_device_ids=true | all-gather | bytes 73728 | tf_op jit(solution)/shard_map/all_gather | solution.py:69
  145.3 0.5 convolution_multiply_fusion
  145.8 1.1 fusion.24
  146.9 0.0 reduce-scatter.5.cloned.1.call-update
  147.0 60.8 %reduce-scatter.5.cloned.1.call-done = f32[16,128]{1,0:T(8,128)} async-done(((f32[128,128]{1,0:T(8,128)}), f32[16,128]{1,0:T(8,128)}) %reduce-scatter.5.cloned.1.call-update) | async-done | bytes 8208 | tf_op jit(solution)/shard_map/reduce_scatter | solution.py:39
  207.7 5.9 %psum.26 = f32[16,128]{1,0:T(8,128)S(1)} all-reduce(f32[16,128]{1,0:T(8,128)} %reduce-scatter.5.cloned.1.call-done), channel_id=1, replica_groups=mesh['dp'=8,'bank'=4] {'bank'}, use_global_device_ids=true, to_apply=%region_14.15 | all-reduce | flops 2048 | bytes 16384 | tf_op jit(solution)/shard_map/psum | solution.py:38
  213.6 0.3 multiply_reduce_fusion.1
  213.9 0.7 subtract_divide_fusion
  (13 shorter events, 0.1 us)
Async XLA Ops:
  7.2 34.5 %copy-start = (f32[512,128]{1,0:T(8,128)S(1)}, f32[512,128]{1,0:T(8,128)}, u32[]{:S(2)}) copy-start(f32[512,128]{1,0:T(8,128)} %param.6) | copy-start | bytes 786436
  7.2 98.6 %reduce-scatter.3.cloned.1.call-start = ((), (), s32[]{:S(2)}) async-start(), calls=%async_computation.2 | async-start | bytes 73728 | tf_op jit(solution)/shard_map/reduce_scatter | solution.py:39
  8.1 1.1 copy-start.1
  43.4 164.3 %reduce-scatter.5.cloned.1.call-start = ((), (), s32[]{:S(2)}) async-start(), calls=%async_computation.3 | async-start | bytes 73728 | tf_op jit(solution)/shard_map/reduce_scatter | solution.py:39
  43.5 0.7 copy-start.4
  111.9 0.7 copy-start.2
  112.8 0.7 copy-start.3
Sparse Core Ops, SparseCore 0:
  43.5 62.1 reduce-scatter.2
  147.1 60.5 reduce-scatter.4
where the time goes:
time: 222 us; the launch traced here: 221 us
  waiting for transfers between devices  99.8 us (45%)
  blocking collectives  95.9 us (43%)
  between operations  14.8 us (7%)
  matrix products  5.06 us (2%)
  other arithmetic  3.32 us (1%)
  local copies, waits for them, and re-layouts  2.43 us (1%)
    reduce_scatter x2, waiting for transfers between devices, reduce_owner(): return lax.psum_scatter(whole, 'dp', scatter_dimension=0, tiled=True)  99.7 us
    all_gather x1, blocking collectives, shards(): gathered = lax.all_gather(normed, 'dp', axis=0, tiled=True)  32.3 us
    all_gather x1, blocking collectives, shards(): gathered_grad = lax.all_gather(grad_soft, 'dp', axis=0, tiled=True)  30.5 us
    unnamed x1, blocking collectives  21.3 us
    psum x2, blocking collectives, reduce_owner(): whole = lax.psum(partials, 'bank')  11.8 us
  transfers between devices with their start and end apart: 2, of which 2 were waited for; matrix products, arithmetic and copies ran while one was open for 0% of the time, Pallas kernels for 0%

commit v1 on v0

--- a/solution.py
+++ b/solution.py
@@ -7,6 +7,22 @@
 EPSILON = 1e-06
 TAU_BACK = 0.1
 HIGHEST = lax.Precision.HIGHEST
+
+
+def ring_gather(x, axis, dim):
+    ways, here, step = (lax.axis_size(axis), lax.axis_index(axis), x.shape[dim])
+    dims = [n * ways if d == dim else n for d, n in enumerate(x.shape)]
+    full = lax.dynamic_update_slice_in_dim(jnp.zeros(dims, x.dtype), x, here * step, axis=dim)
+    going_up = going_down = x
+    for far in range(1, ways // 2 + 1):
+        going_up = lax.ppermute(going_up, axis, [(d, (d + 1) % ways) for d in range(ways)])
+        full = lax.dynamic_update_slice_in_dim(full, going_up, (here - far) % ways * step, axis=dim)
+        if 2 * far < ways:
+            going_down = lax.ppermute(going_down, axis, [(d, (d - 1) % ways) for d in range(ways)])
+            full = lax.dynamic_update_slice_in_dim(
+                full, going_down, (here + far) % ways * step, axis=dim
+            )
+    return full
 
 
 def unit_rows(values):
@@ -66,7 +82,7 @@
         normed,
     )
     grad_soft, grad_local = pullback(loss_weight)
-    gathered_grad = lax.all_gather(grad_soft, "dp", axis=0, tiled=True)
+    gathered_grad = ring_gather(grad_soft, "dp", 0)
     grad_blocks = gathered_grad.reshape(-1, step_rows, width)
 
     def backward_block(paired):

time: 222 us -> 215 us (0.968)
  blocking collectives: 95.9 us -> 65.4 us
  starting transfers between devices: 0.08 us -> 14.3 us
  waiting for transfers between devices: 99.8 us -> 109 us
    all_gather x1 -> x0, blocking collectives: 30.5 us -> none  [shards(): gathered_grad = lax.all_gather(grad_soft, 'dp', axis=0, tiled=True)]
    ppermute x0 -> x7, starting transfers between devices: none -> 14.2 us  [the longest x3 12.7 us: ring_gather(): lax.ppermute(going_down, axis, [(d, (d - 1) % ways) for d in range(ways)])]
    ppermute x0 -> x7, waiting for transfers between devices: none -> 11.2 us  [the longest x4 11.2 us: ring_gather(): lax.ppermute(going_up, axis, [(d, (d + 1) % ways) for d in range(ways)])]
  transfers between devices with their start and end apart: 2 -> 9, of which waited for: 2 -> 6; matrix products, arithmetic and copies ran while one was open for 0% -> 0% of each run, Pallas kernels for 0% -> 0%
where the time goes in v1:
time: 215 us
  waiting for transfers between devices  109 us (51%)
  blocking collectives  65.4 us (30%)
  between operations  14.8 us (7%)
  starting transfers between devices  14.3 us (7%)
  matrix products  5.06 us (2%)
  other arithmetic  3.32 us (2%)
  local copies, waits for them, and re-layouts  2.46 us (1%)
    reduce_scatter x2, waiting for transfers between devices, reduce_owner(): return lax.psum_scatter(whole, 'dp', scatter_dimension=0, tiled=True)  98 us
    all_gather x1, blocking collectives, shards(): gathered = lax.all_gather(normed, 'dp', axis=0, tiled=True)  32.3 us
    unnamed x1, blocking collectives  21.3 us
    ppermute x3, starting transfers between devices, ring_gather(): lax.ppermute(going_down, axis, [(d, (d - 1) % ways) for d in range(ways)])  12.7 us
    psum x2, blocking collectives, reduce_owner(): whole = lax.psum(partials, 'bank')  11.8 us
    ppermute x4, waiting for transfers between devices, ring_gather(): lax.ppermute(going_up, axis, [(d, (d + 1) % ways) for d in range(ways)])  11.2 us
  transfers between devices with their start and end apart: 9, of which 6 were waited for; matrix products, arithmetic and copies ran while one was open for 0% of the time, Pallas kernels for 0%

profile of v1, /device:TPU:0, one launch (start us, length us, event | category | flops | bytes accessed | tf_op | source)
XLA Modules:
  0.0 214.6 jit_solution(10557999358120872976)
XLA Ops:
  7.2 0.8 multiply_reduce_fusion.6
  8.1 1.1 multiply_reduce_fusion
  9.4 32.3 %all_gather.3 = f32[128,128]{1,0:T(8,128)S(1)} all-gather(f32[16,128]{1,0:T(8,128)S(1)} %get-tuple-element.42), channel_id=1, replica_groups=mesh['dp'=8,'bank'=4] {'dp'}, dimensions={0}, use_global_device_ids=true | all-gather | bytes 73728 | tf_op jit(solution)/shard_map/all_gather | solution.py:65
  41.7 0.6 fusion.28
  42.3 1.1 fusion.25
  43.5 0.6 copy-done.4
  44.1 0.6 dynamic-slice.1
  45.4 21.3 %all-reduce = f32[128]{0:T(128)S(1)} all-reduce(f32[128]{0:T(128)S(1)} %get-tuple-element.47), channel_id=3, replica_groups=mesh['dp'=8,'bank'=4] {'dp'}, use_global_device_ids=true, to_apply=%region_7.8.clone | all-reduce | flops 128 | bytes 1024
  66.7 39.0 %reduce-scatter.3.cloned.1.call-done = f32[16,128]{1,0:T(8,128)} async-done(((f32[128,128]{1,0:T(8,128)}), f32[16,128]{1,0:T(8,128)}) %reduce-scatter.3.cloned.1.call-update) | async-done | bytes 8208 | tf_op jit(solution)/shard_map/reduce_scatter | solution.py:55
  105.7 6.0 %all-reduce.1 = (f32[16,128]{1,0:T(8,128)S(1)}, f32[16]{0:T(128)S(1)}) all-reduce(f32[16,128]{1,0:T(8,128)} %reduce-scatter.3.cloned.1.call-done, f32[16]{0:T(128)S(1)} %dynamic-slice.2), channel_id=1, replica_groups=mesh['dp'=8,'bank'=4] {'bank'}, use_global_device_ids=true, to_apply=%region_3.0 | all-reduce | flops 2064 | bytes 16512 | tf_op jit(solution)/shard_map/psum | solution.py:54
  111.7 0.2 multiply_reduce_fusion.5
  111.9 0.7 copy-done.2
  112.6 0.2 fusion.12
  112.8 0.2 convolution_bitcast_fusion.1
  113.0 0.5 copy-done.3
  113.5 0.7 add_add_fusion
  114.3 0.2 multiply_reduce_fusion.8
  114.5 0.3 multiply_reduce_fusion.2
  114.8 1.5 collective-permute-start
  116.4 3.3 %collective-permute-start.1 = (f32[16,128]{1,0:T(8,128)S(1)}, f32[16,128]{1,0:T(8,128)S(1)}, u32[]{:S(2)}, u32[]{:S(2)}) collective-permute-start(f32[16,128]{1,0:T(8,128)S(1)} %get-tuple-element.50), channel_id=1, source_target_pairs={{0,28},{4,0},{8,4},{12,8},{16,12},{20,16},{24,20},{28,24},{1,29},{... | collective-permute-start | bytes 24584 | tf_op jit(solution)/shard_map/ppermute | solution.py:21
  119.6 1.6 collective-permute-done
  121.2 4.7 %collective-permute-start.3 = (f32[16,128]{1,0:T(8,128)S(1)}, f32[16,128]{1,0:T(8,128)S(1)}, u32[]{:S(2)}, u32[]{:S(2)}) collective-permute-start(f32[16,128]{1,0:T(8,128)S(1)} %collective-permute-done.1), channel_id=1, source_target_pairs={{0,28},{4,0},{8,4},{12,8},{16,12},{20,16},{24,20},{28,24},{1,29},{... | collective-permute-start | bytes 24584 | tf_op jit(solution)/shard_map/ppermute | solution.py:21
  126.0 1.6 collective-permute-done.2
  127.6 4.7 %collective-permute-start.5 = (f32[16,128]{1,0:T(8,128)S(1)}, f32[16,128]{1,0:T(8,128)S(1)}, u32[]{:S(2)}, u32[]{:S(2)}) collective-permute-start(f32[16,128]{1,0:T(8,128)S(1)} %collective-permute-done.3), channel_id=1, source_target_pairs={{0,28},{4,0},{8,4},{12,8},{16,12},{20,16},{24,20},{28,24},{1,29},{... | collective-permute-start | bytes 24584 | tf_op jit(solution)/shard_map/ppermute | solution.py:21
  132.3 1.6 collective-permute-done.4
  134.0 6.3 %collective-permute-done.6 = f32[16,128]{1,0:T(8,128)S(1)} collective-permute-done((f32[16,128]{1,0:T(8,128)S(1)}, f32[16,128]{1,0:T(8,128)S(1)}, u32[]{:S(2)}, u32[]{:S(2)}) %collective-permute-start.6) | collective-permute-done | bytes 8224 | tf_op jit(solution)/shard_map/ppermute | solution.py:18
  140.3 0.5 convolution_multiply_fusion
  140.8 1.1 fusion.24
  141.9 59.0 %reduce-scatter.5.cloned.1.call-done = f32[16,128]{1,0:T(8,128)} async-done(((f32[128,128]{1,0:T(8,128)}), f32[16,128]{1,0:T(8,128)}) %reduce-scatter.5.cloned.1.call-update) | async-done | bytes 8208 | tf_op jit(solution)/shard_map/reduce_scatter | solution.py:55
  200.9 5.9 %psum.26 = f32[16,128]{1,0:T(8,128)S(1)} all-reduce(f32[16,128]{1,0:T(8,128)} %reduce-scatter.5.cloned.1.call-done), channel_id=1, replica_groups=mesh['dp'=8,'bank'=4] {'bank'}, use_global_device_ids=true, to_apply=%region_14.15 | all-reduce | flops 2048 | bytes 16384 | tf_op jit(solution)/shard_map/psum | solution.py:54
  206.7 0.3 multiply_reduce_fusion.1
  207.1 0.7 subtract_divide_fusion
  (34 shorter events, 0.6 us)
Async XLA Ops:
  7.2 34.5 %copy-start = (f32[512,128]{1,0:T(8,128)S(1)}, f32[512,128]{1,0:T(8,128)}, u32[]{:S(2)}) copy-start(f32[512,128]{1,0:T(8,128)} %param.6) | copy-start | bytes 786436
  7.2 98.6 %reduce-scatter.3.cloned.1.call-start = ((), (), s32[]{:S(2)}) async-start(), calls=%async_computation.2 | async-start | bytes 73728 | tf_op jit(solution)/shard_map/reduce_scatter | solution.py:55
  8.1 1.1 copy-start.1
  43.4 157.5 %reduce-scatter.5.cloned.1.call-start = ((), (), s32[]{:S(2)}) async-start(), calls=%async_computation.3 | async-start | bytes 73728 | tf_op jit(solution)/shard_map/reduce_scatter | solution.py:55
  43.5 0.7 copy-start.4
  111.9 0.7 copy-start.2
  112.8 0.7 copy-start.3
  114.8 6.4 %collective-permute-start = (f32[16,128]{1,0:T(8,128)S(1)}, f32[16,128]{1,0:T(8,128)S(1)}, u32[]{:S(2)}, u32[]{:S(2)}) collective-permute-start(f32[16,128]{1,0:T(8,128)S(1)} %get-tuple-element.50), channel_id=1, source_target_pairs={{0,4},{4,8},{8,12},{12,16},{16,20},{20,24},{24,28},{28,0},{1,5},{5... | collective-permute-start | bytes 24584 | tf_op jit(solution)/shard_map/ppermute | solution.py:18
  116.4 4.9 %collective-permute-start.1 = (f32[16,128]{1,0:T(8,128)S(1)}, f32[16,128]{1,0:T(8,128)S(1)}, u32[]{:S(2)}, u32[]{:S(2)}) collective-permute-start(f32[16,128]{1,0:T(8,128)S(1)} %get-tuple-element.50), channel_id=1, source_target_pairs={{0,28},{4,0},{8,4},{12,8},{16,12},{20,16},{24,20},{28,24},{1,29},{... | collective-permute-start | bytes 24584 | tf_op jit(solution)/shard_map/ppermute | solution.py:21
  121.2 6.3 %collective-permute-start.2 = (f32[16,128]{1,0:T(8,128)S(1)}, f32[16,128]{1,0:T(8,128)S(1)}, u32[]{:S(2)}, u32[]{:S(2)}) collective-permute-start(f32[16,128]{1,0:T(8,128)S(1)} %collective-permute-done), channel_id=1, source_target_pairs={{0,4},{4,8},{8,12},{12,16},{16,20},{20,24},{24,28},{28,0},{1,5},{5... | collective-permute-start | bytes 24584 | tf_op jit(solution)/shard_map/ppermute | solution.py:18
  121.2 6.3 %collective-permute-start.3 = (f32[16,128]{1,0:T(8,128)S(1)}, f32[16,128]{1,0:T(8,128)S(1)}, u32[]{:S(2)}, u32[]{:S(2)}) collective-permute-start(f32[16,128]{1,0:T(8,128)S(1)} %collective-permute-done.1), channel_id=1, source_target_pairs={{0,28},{4,0},{8,4},{12,8},{16,12},{20,16},{24,20},{28,24},{1,29},{... | collective-permute-start | bytes 24584 | tf_op jit(solution)/shard_map/ppermute | solution.py:21
  127.6 6.3 %collective-permute-start.4 = (f32[16,128]{1,0:T(8,128)S(1)}, f32[16,128]{1,0:T(8,128)S(1)}, u32[]{:S(2)}, u32[]{:S(2)}) collective-permute-start(f32[16,128]{1,0:T(8,128)S(1)} %collective-permute-done.2), channel_id=1, source_target_pairs={{0,4},{4,8},{8,12},{12,16},{16,20},{20,24},{24,28},{28,0},{1,5},{5... | collective-permute-start | bytes 24584 | tf_op jit(solution)/shard_map/ppermute | solution.py:18
  127.6 6.3 %collective-permute-start.5 = (f32[16,128]{1,0:T(8,128)S(1)}, f32[16,128]{1,0:T(8,128)S(1)}, u32[]{:S(2)}, u32[]{:S(2)}) collective-permute-start(f32[16,128]{1,0:T(8,128)S(1)} %collective-permute-done.3), channel_id=1, source_target_pairs={{0,28},{4,0},{8,4},{12,8},{16,12},{20,16},{24,20},{28,24},{1,29},{... | collective-permute-start | bytes 24584 | tf_op jit(solution)/shard_map/ppermute | solution.py:21
  133.9 6.3 %collective-permute-start.6 = (f32[16,128]{1,0:T(8,128)S(1)}, f32[16,128]{1,0:T(8,128)S(1)}, u32[]{:S(2)}, u32[]{:S(2)}) collective-permute-start(f32[16,128]{1,0:T(8,128)S(1)} %collective-permute-done.4), channel_id=1, source_target_pairs={{0,4},{4,8},{8,12},{12,16},{16,20},{20,24},{24,28},{28,0},{1,5},{5... | collective-permute-start | bytes 24584 | tf_op jit(solution)/shard_map/ppermute | solution.py:18
Sparse Core Ops, SparseCore 0:
  43.5 62.1 reduce-scatter.2
  142.0 58.8 reduce-scatter.4
